TPU v7x, 256 devices: a whole 4x4x8 slice. The times are simulated.
256 devices in a mesh: section: 16 (over z_lo, y), dp: 2 (over core), tensor: 8 (over z_hi, x).
Axes of the slice: x: 4, y: 4, z: 8 (z_hi: 2, z_lo: 4; z = z_hi * 4 + z_lo), core: 2. Of those that a mesh axis runs over, the one named last changes fastest.
Arguments:
- partials: bfloat16 [16, 8, 256, 16384], P('section', 'tensor', 'dp'), parts along dimension 2, may hold values from -3 to 3
- residual: bfloat16 [16, 256, 16384], P('section', 'dp', 'tensor'), parts along dimension 1, may hold values from -48 to 48
- exponents: int32 [16, 256, 128], P('section', 'dp', 'tensor'), parts along dimension 1, may hold values from -8 to -4
- signs: int32 [16384], replicated, may hold values from 0 to 1
- gain: float32 [16384], replicated, may hold values from 0.1 to 1.9
- kv_weight: bfloat16 [16, 2, 16384, 1024], P('section', None, None, 'tensor'), may hold values from -0.046875 to 0.046875
Outputs:
- keys_values: bfloat16 [16, 2, 256, 1024], P('section', None, 'dp', 'tensor'), parts along dimension 2
There are 2 independent parts, one for each index of `dp`. A program takes and returns all parts, laid end to end along the dimension named above; an argument that names none is the same for every part. Nothing has to cross between parts.
Inputs may be any that keep to these rules, and one draw needn't show every extreme that they name: `exponents`: scale exponent of each block of 128 features of a token. `signs`: sign bits, 1 for plus.
All inputs are finite; a program needn't handle non-finite values.
Results may differ from a plain program's by a relative error of at most 0.019.
Values may be sent and summed in bfloat16 or wider, within the bound.
A program may use at most 128 MiB of HBM per device.

v0:
```python
import math

import jax
import jax.numpy as jnp
from jax import lax
from jax.sharding import PartitionSpec as P

BLOCK = 128


clip_level = 448.0
exp_low = -8
exp_high = -3
norm_eps = 1e-05


def shifted(x, axis, by):
    peers = lax.axis_size(axis)
    pairs = [(i, i + by) for i in range(peers) if 0 <= i + by < peers]
    return lax.ppermute(x, axis, pairs)


def rotation(order_size):
    rows_i = jnp.arange(order_size, dtype=jnp.int32)[:, None]
    cols_j = jnp.arange(order_size, dtype=jnp.int32)[None, :]
    parity = jnp.zeros((order_size, order_size), jnp.int32)
    level = 1
    while level < order_size:
        parity = parity + rows_i // level % 2 * (cols_j // level % 2)
        level = level * 2
    sign_h = (1 - 2 * (parity % 2)).astype(jnp.float32)
    return sign_h * jnp.float32(1.0 / math.sqrt(order_size))


def power_table(exponents_in, direction):
    factor = jnp.zeros(exponents_in.shape, jnp.float32)
    for power_level in range(exp_low, exp_high):
        factor = factor + jnp.where(
            exponents_in == power_level,
            jnp.float32(2.0 ** (direction * power_level)),
            jnp.float32(0.0),
        )
    return factor


def encode(summed, exponents_in, sign_vals, matrix_h):
    rows_n, cols_n = summed.shape
    blk = matrix_h.shape[0]
    shaped = (summed * sign_vals).reshape(rows_n, cols_n // blk, blk)
    turned = jnp.einsum("tbk,kj->tbj", shaped, matrix_h, precision=lax.Precision.HIGHEST)
    scaled = turned * power_table(exponents_in, -1)[:, :, None]
    return jnp.clip(scaled, -clip_level, clip_level).astype(jnp.bfloat16).reshape(rows_n, cols_n)


def decode(coded, exponents_in, sign_vals, matrix_h):
    rows_n, cols_n = coded.shape
    blk = matrix_h.shape[0]
    shaped = (
        coded.astype(jnp.float32).reshape(rows_n, cols_n // blk, blk)
        * power_table(exponents_in, 1)[:, :, None]
    )
    turned = jnp.einsum("tbk,kj->tbj", shaped, matrix_h, precision=lax.Precision.HIGHEST)
    return turned.reshape(rows_n, cols_n) * sign_vals


def normalize(decoded, gain):
    meansq = jnp.mean(decoded * decoded, axis=1, keepdims=True)
    return (decoded * lax.rsqrt(meansq + norm_eps) * gain).astype(jnp.bfloat16)


def on_device(partials, residual, exponents, signs, gain, kv_weight):
    matrix_h = rotation(BLOCK)
    sign_all = (2 * signs - 1).astype(jnp.float32)
    local_cols = residual.shape[2]
    offset = lax.axis_index("tensor") * local_cols
    sign_own = lax.dynamic_slice_in_dim(sign_all, offset, local_cols, 0)
    branch = lax.psum_scatter(
        partials[0, 0].astype(jnp.float32).astype(jnp.bfloat16),
        "tensor",
        scatter_dimension=1,
        tiled=True,
    ).astype(jnp.float32)
    summed = residual[0].astype(jnp.float32) + branch
    expo_own = exponents[0]
    coded = encode(summed, expo_own, sign_own, matrix_h)
    got_coded, got_expo = shifted((coded, expo_own), "section", 1)
    full_coded, full_expo = (
        lax.all_gather(got_coded, "tensor", axis=1, tiled=True),
        lax.all_gather(got_expo, "tensor", axis=1, tiled=True),
    )
    normed = normalize(decode(full_coded, full_expo, sign_all, matrix_h), gain)
    result = jnp.einsum("td,cdh->cth", normed, kv_weight[0], preferred_element_type=jnp.float32)
    return result.astype(jnp.bfloat16)[None]


def solution(mesh):
    placed = (
        P("section", "tensor", "dp", None),
        P("section", "dp", "tensor"),
        P("section", "dp", "tensor"),
        P(),
        P(),
        P("section", None, None, "tensor"),
    )
    return jax.shard_map(
        on_device,
        mesh=mesh,
        in_specs=placed,
        out_specs=P("section", None, "dp", "tensor"),
        check_vma=False,
    )
```

profile of v0, /device:TPU:34, one launch (start us, length us, event | category | flops | bytes accessed | tf_op | source)
XLA Modules:
  0.0 300.1 jit_solution(13410715496880103278)
XLA Ops:
  6.5 0.0 reduce-scatter.2.cloned.1.call-start
  6.5 0.7 reduce-scatter.2.cloned.1.call-update
  7.3 0.0 all-gather.2.cloned.1.call-start
  7.3 0.9 fusion.70
  8.2 0.7 select_add_fusion.1
  8.9 130.8 %reduce-scatter.2.cloned.1.call-done = bf16[128,2048]{1,0:T(8,128)(2,1)} async-done(((bf16[128,16384]{1,0:T(8,128)(2,1)}), bf16[128,2048]{1,0:T(8,128)(2,1)}) %reduce-scatter.2.cloned.1.call-update) | async-done | bytes 524304 | tf_op jit(solution)/shard_map/reduce_scatter | solution.py:77
  139.7 2.6 fusion.6
  142.3 3.4 %collective-permute-start = (bf16[128,2048]{0,1:T(8,128)(2,1)S(1)}, bf16[128,2048]{0,1:T(8,128)(2,1)S(1)}, u32[]{:S(2)}, u32[]{:S(2)}) collective-permute-start(bf16[128,2048]{0,1:T(8,128)(2,1)S(1)} %bitcast.44), channel_id=1, source_target_pairs={{0,16},{16,32},{32,48},{48,64},{64,80},{80,96},{96,112},{112,128},... | collective-permute-start | bytes 1572872 | tf_op jit(solution)/shard_map/ppermute | solution.py:20
  145.7 12.4 %collective-permute-done = bf16[128,2048]{0,1:T(8,128)(2,1)S(1)} collective-permute-done((bf16[128,2048]{0,1:T(8,128)(2,1)S(1)}, bf16[128,2048]{0,1:T(8,128)(2,1)S(1)}, u32[]{:S(2)}, u32[]{:S(2)}) %collective-permute-start) | collective-permute-done | bytes 524320 | tf_op jit(solution)/shard_map/ppermute | solution.py:20
  158.1 0.0 copy-start
  158.1 0.8 copy-done
  158.9 0.0 all-gather.2.cloned.1.call-update
  158.9 1.9 collective-permute-start.1
  160.9 5.9 %collective-permute-done.1 = s32[128,16]{0,1:T(8,128)S(1)} collective-permute-done((s32[128,16]{0,1:T(8,128)}, s32[128,16]{0,1:T(8,128)S(1)}, u32[]{:S(2)}, u32[]{:S(2)}) %collective-permute-start.1) | collective-permute-done | bytes 8224 | tf_op jit(solution)/shard_map/ppermute | solution.py:20
  166.8 39.9 %all_gather.7 = s32[128,128]{0,1:T(8,128)S(1)} all-gather(s32[128,16]{0,1:T(8,128)S(1)} %collective-permute-done.1), channel_id=1, replica_groups=mesh['section'=16,'dp'=2,'tensor'=8] {'tensor'}, dimensions={1}, use_global_device_ids=true | all-gather | bytes 73728 | tf_op jit(solution)/shard_map/all_gather | solution.py:89
  206.8 0.1 copy.10
  206.9 52.2 %all-gather.2.cloned.1.call-done = bf16[128,16384]{0,1:T(8,128)(2,1)} async-done(((bf16[128,2048]{0,1:T(8,128)(2,1)}), bf16[128,16384]{0,1:T(8,128)(2,1)}) %all-gather.2.cloned.1.call-update) | async-done | bytes 4194320 | tf_op jit(solution)/shard_map/all_gather | solution.py:88
  259.1 6.9 %copy.13 = f32[128,128,128]{2,1,0:T(8,128)} copy(bf16[128,128,128]{0,2,1:T(8,128)(2,1)} %bitcast.40) | data formatting | bytes 12582912 | tf_op jit(solution)/shard_map/reshape | solution.py:59
  266.0 0.0 copy-start.1
  266.0 10.1 %multiply_reduce_fusion = (f32[128]{0:T(128)S(1)}, f32[128,128,128]{2,1,0:T(8,128)S(1)}) fusion(f32[128,128]{1,0:T(8,128)S(1)} %get-tuple-element.5, s32[128]{0:T(128)S(1)} %get-tuple-element.9, s32[128]{0:T(128)S(1)} %get-tuple-element.10, s32[128]{0:T(128)S(1)} %get-tuple-element.11, s32[128]{0:T(128)S(1)} %get-tuple-element.12, ...), kind=kOutput, calls=%fused_computation.3 | convolution fusion | flops 3230072832 | bytes 16912384 | tf_op jit(solution)/shard_map/tbk,kj->tbj/dot_general | solution.py:62
  276.1 0.0 copy-done.1
  276.2 3.2 %multiply_convert_fusion = bf16[128,128,128]{2,1,0:T(8,128)(2,1)} fusion(f32[128,128,128]{2,1,0:T(8,128)S(1)} %get-tuple-element.8, f32[128,128]{1,0:T(8,128)S(1)} %bitcast.42, f32[128]{0:T(128)S(1)} %add_rsqrt_fusion, f32[128,128]{1,0:T(8,128)S(1)} %get-tuple-element.5), kind=kLoop, calls=%fused_computation.2 | loop fusion | flops 8388608 | bytes 12714496 | tf_op jit(solution)/shard_map/convert_element_type | solution.py:68
  279.4 7.3 %reshape.744 = bf16[128,16384,1]{1,0,2:T(8,128)(2,1)} reshape(bf16[128,128,128]{2,1,0:T(8,128)(2,1)} %multiply_convert_fusion) | data formatting | bytes 8388608 | tf_op jit(solution)/shard_map/convert_element_type | solution.py:68
  286.7 6.5 %fusion.10 = bf16[1,2,128,128]{3,2,1,0:T(8,128)(2,1)} fusion(bf16[128,16384,1]{1,0,2:T(8,128)(2,1)} %reshape.744, bf16[1,2,16384,128]{3,2,1,0:T(8,128)(2,1)} %param.11), kind=kOutput, calls=%fused_computation.11 | convolution fusion | flops 1073774592 | bytes 12648448 | tf_op jit(solution)/shard_map/td,cdh->cth/dot_general | solution.py:92
  (7 shorter events, 0.1 us)
Async XLA Ops:
  6.5 133.2 %reduce-scatter.2.cloned.1.call-start = ((), (), s32[]{:S(2)}) async-start(), calls=%async_computation.1 | async-start | bytes 4718592 | tf_op jit(solution)/shard_map/reduce_scatter | solution.py:77
  7.3 251.8 %all-gather.2.cloned.1.call-start = ((), (), s32[]{:S(2)}) async-start(), calls=%async_computation.2 | async-start | bytes 4718592 | tf_op jit(solution)/shard_map/all_gather | solution.py:88
  142.3 15.8 %collective-permute-start = (bf16[128,2048]{0,1:T(8,128)(2,1)S(1)}, bf16[128,2048]{0,1:T(8,128)(2,1)S(1)}, u32[]{:S(2)}, u32[]{:S(2)}) collective-permute-start(bf16[128,2048]{0,1:T(8,128)(2,1)S(1)} %bitcast.44), channel_id=1, source_target_pairs={{0,16},{16,32},{32,48},{48,64},{64,80},{80,96},{96,112},{112,128},... | collective-permute-start | bytes 1572872 | tf_op jit(solution)/shard_map/ppermute | solution.py:20
  158.1 0.8 copy-start
  158.9 7.9 %collective-permute-start.1 = (s32[128,16]{0,1:T(8,128)}, s32[128,16]{0,1:T(8,128)S(1)}, u32[]{:S(2)}, u32[]{:S(2)}) collective-permute-start(s32[128,16]{0,1:T(8,128)} %bitcast.43), channel_id=1, source_target_pairs={{0,16},{16,32},{32,48},{48,64},{64,80},{80,96},{96,112},{112,128},... | collective-permute-start | bytes 24584 | tf_op jit(solution)/shard_map/ppermute | solution.py:20
  266.0 10.2 %copy-start.1 = (f32[16384]{0:T(1024)S(1)}, f32[16384]{0:T(1024)}, u32[]{:S(2)}) copy-start(f32[16384]{0:T(1024)} %param.10) | copy-start | bytes 196612
Sparse Core Ops, SparseCore 0:
  11.5 128.1 reduce-scatter.1
  159.1 99.9 all-gather.1
where the time goes:
time: 304 us; the launch traced here: 300 us
  waiting for transfers between devices  202 us (66%)
  blocking collectives  39.9 us (13%)
  matrix products  19.3 us (6%)
  local copies, waits for them, and re-layouts  15.2 us (5%)
  between operations  13.5 us (4%)
  starting transfers between devices  5.36 us (2%)
  other arithmetic  4.86 us (2%)
    reduce_scatter x1, waiting for transfers between devices, on_device(): lax.psum_scatter(partials[0, 0].astype(jnp.float32).astype(jnp.bfloat16),...  131 us
    all_gather x1, waiting for transfers between devices, on_device(): lax.all_gather(got_coded, 'tensor', axis=1, tiled=True)  52.2 us
    all_gather x1, blocking collectives, on_device(): lax.all_gather(got_expo, 'tensor', axis=1, tiled=True)  39.9 us
    ppermute x2, waiting for transfers between devices, shifted(): return lax.ppermute(x, axis, pairs)  18.4 us
    dot_general x1, matrix products, decode(): jnp.einsum('tbk,kj->tbj', shaped, matrix_h, precision=lax.Precision.HIGHEST)  10.1 us
    convert_element_type x1, local copies, waits for them, and re-layouts, normalize(): return (decoded * lax.rsqrt(meansq + norm_eps) * gain).astype(jnp.bfloat16)  7.35 us
    reshape x1, local copies, waits for them, and re-layouts, decode(): coded.astype(jnp.float32).reshape(rows_n, cols_n // blk, blk)  6.94 us
    dot_general x1, matrix products, on_device(): jnp.einsum('td,cdh->cth', normed, kv_weight[0], preferred_element_type=jn...  6.54 us
  transfers between devices with their start and end apart: 4, of which 4 were waited for; matrix products, arithmetic and copies ran while one was open for 1% of the time, Pallas kernels for 0%

commit v1 on v0

v1 whole, which is shorter than its diff:
```python
import functools
import math

import jax
import jax.numpy as jnp
from jax import lax
from jax.experimental import pallas as pl
from jax.experimental.pallas import tpu as pltpu
from jax.sharding import PartitionSpec as P

MESH = pl.DeviceIdType.MESH
BLOCK = 128
clip_level = 448.0
exp_low = -8
exp_high = -3
norm_eps = 1e-05
SLICES = 8
NX = 4


def power_table(exponents_in, direction):
    factor = jnp.zeros(exponents_in.shape, jnp.float32)
    for power_level in range(exp_low, exp_high):
        factor = factor + jnp.where(
            exponents_in == power_level,
            jnp.float32(2.0 ** (direction * power_level)),
            jnp.float32(0.0),
        )
    return factor


def hadamard_signs(rows, cols):
    i = lax.broadcasted_iota(jnp.int32, (rows, cols), 0)
    j = lax.broadcasted_iota(jnp.int32, (rows, cols), 1)
    p = (i & j) & (BLOCK - 1)
    p = p ^ (p >> 4)
    p = p ^ (p >> 2)
    p = p ^ (p >> 1)
    signs = (1 - 2 * (p & 1)).astype(jnp.float32)
    return jnp.where((i >> 7) == (j >> 7), signs, 0.0)


def kernel(
    part, resid, expo_h, signs_h, gain_h, w_h, out,
    pv, ab, rsb, zs, zr, ys, g, wv, wp, rv, expo, signs, gain, h_one, h_two, acc, ssq,
    pv_s, in_s, a_s, a_r, raw_s, comb_s, rs_r, z_s, z_r, y_s, y_r, ag_s, ag_r, fw_s, fw_r,
):
    n_sec = lax.axis_size("section")
    s, dp, t = lax.axis_index("section"), lax.axis_index("dp"), lax.axis_index("tensor")
    zh, x = t // NX, t % NX
    xr, xl, xo = (x + 1) % NX, (x + 3) % NX, (x + 2) % NX
    tok, slices, width = pv.shape[2], pv.shape[1], pv.shape[3]
    own = slices * width
    blocks = width // BLOCK
    norm_h = jnp.float32(1.0 / math.sqrt(BLOCK))

    def at(section, z_hi, col):
        return (section, dp, z_hi * NX + col)

    right, left, across = at(s, zh, xr), at(s, zh, xl), at(s, 1 - zh, x)

    def cols(z_hi, col, j):
        return pl.ds(pl.multiple_of((z_hi * NX + col) * own + j * width, width), width)

    own_loads = []
    for j in range(slices):
        for k, (z_hi, col) in enumerate(((0, xr), (1, xl), (0, x), (1, x))):
            own_loads.append(
                pltpu.make_async_copy(part.at[0, 0, :, cols(z_hi, col, j)], pv.at[k, j], pv_s.at[k, j])
            )
    small = [
        pltpu.make_async_copy(expo_h.at[0], expo, in_s.at[0]),
        pltpu.make_async_copy(signs_h, signs, in_s.at[1]),
        pltpu.make_async_copy(gain_h, gain, in_s.at[2]),
        pltpu.make_async_copy(resid.at[0], rv, in_s.at[3]),
        pltpu.make_async_copy(w_h.at[0, 0], wv.at[0], in_s.at[4]),
        pltpu.make_async_copy(w_h.at[0, 1], wv.at[1], in_s.at[5]),
    ]
    for c in own_loads[:8]:
        c.start()
    for c in small:
        c.start()
    for c in own_loads[8:]:
        c.start()

    bar = pltpu.get_barrier_semaphore()

    def greet(device):
        pl.semaphore_signal(bar, inc=1, device_id=device, device_id_type=MESH)

    for device in (right, left, across):
        greet(device)

    @pl.when(s > 0)
    def _():
        greet(at(s - 1, 0, x))
        greet(at(s - 1, 1, x))

    @pl.when(s < n_sec - 1)
    def _():
        greet(at(s + 1, 0, x))
        greet(at(s + 1, 1, x))

    before = (s + n_sec - 1) // n_sec
    after = (2 * n_sec - 2 - s) // n_sec
    pl.semaphore_wait(bar, 3 + 2 * before + 2 * after)

    def remote(src, dst, send, recv, device):
        return pltpu.make_async_remote_copy(
            src_ref=src, dst_ref=dst, send_sem=send, recv_sem=recv, device_id=device, device_id_type=MESH
        )

    def far(j, d):
        z_hi, device = (0, right) if d == 0 else (1, left)
        return remote(part.at[0, 0, :, cols(z_hi, xo, j)], ab.at[d, j], a_s.at[d, j], a_r.at[d, j], device)

    def near(j, d):
        z_hi, col, device = (1, xr, right) if d == 0 else (0, xl, left)
        return remote(
            part.at[0, 0, :, cols(z_hi, col, j)], rsb.at[z_hi, d, j], raw_s.at[d, j], rs_r.at[z_hi, d, j], device
        )

    def comb(j, d):
        device = right if d == 0 else left
        return remote(ab.at[d, j], rsb.at[d, d, j], comb_s.at[d, j], rs_r.at[d, d, j], device)

    def pair(j):
        return remote(zs.at[j], zr.at[j], z_s.at[j], z_r.at[j], across)

    def hand(j, z_hi):
        return remote(
            ys.at[j], g.at[x, j, zh], y_s.at[z_hi, j], y_r.at[zh, j], at(s + 1, z_hi, x)
        )

    def gather(j, d, z_hi):
        device = right if d == 0 else left
        return remote(g.at[x, j, z_hi], g.at[x, j, z_hi], ag_s.at[d, z_hi, j], ag_r.at[d, z_hi, j], device)

    def forward(j, d):
        device, col = (right, xl) if d == 0 else (left, xr)
        return remote(g.at[col, j, d], g.at[col, j, d], fw_s.at[d, j], fw_r.at[d, j], device)

    def got_gather(j, d, z_hi):
        col = xl if d == 0 else xr
        remote(g.at[col, j, z_hi], g.at[col, j, z_hi], ag_s.at[d, z_hi, j], ag_r.at[d, z_hi, j], right).wait_recv()

    def got_forward(j, d):
        remote(g.at[xo, j, d], g.at[xo, j, d], fw_s.at[d, j], fw_r.at[d, j], right).wait_recv()

    for d in (0, 1):
        far(0, d).start()
    for d in (0, 1):
        near(0, d).start()
    for d in (0, 1):
        far(1, d).start()

    h_one[...] = hadamard_signs(BLOCK, BLOCK)
    h_two[...] = hadamard_signs(2 * BLOCK, 2 * BLOCK).astype(jnp.bfloat16)
    acc[...] = jnp.zeros_like(acc)
    ssq[...] = jnp.zeros_like(ssq)

    @pl.when(s == 0)
    def _():
        g[x] = jnp.zeros(g.shape[1:], g.dtype)

    def combine(j):
        for d in (0, 1):
            own_loads[4 * j + d].wait()
            far(j, d).wait_recv()
            ab[d, j] = (ab[d, j].astype(jnp.float32) + pv[d, j].astype(jnp.float32)).astype(jnp.bfloat16)
            comb(j, d).start()

    def gathered_sum(j, z_hi):
        return (
            rsb[z_hi, 0, j].astype(jnp.float32)
            + rsb[z_hi, 1, j].astype(jnp.float32)
            + pv[2 + z_hi, j].astype(jnp.float32)
        )

    def exchange(j):
        own_loads[4 * j + 2].wait()
        own_loads[4 * j + 3].wait()
        for d in (0, 1):
            near(j, d).wait_recv()
            comb(j, d).wait_recv()
        zs[j] = gathered_sum(j, 1 - zh).astype(jnp.bfloat16)
        pair(j).start()

    def row(ref, b):
        return ref[pl.ds(b, 1), :]

    def encode(j):
        pair(j).wait_recv()
        summed = (
            gathered_sum(j, zh)
            + zr[j].astype(jnp.float32)
            + rv[:, j * width : (j + 1) * width].astype(jnp.float32)
        )
        e = expo[...]
        for q in range(0, blocks, 2):
            b = t * (own // BLOCK) + j * blocks + q
            sgn = jnp.concatenate([row(signs, b), row(signs, b + 1)], axis=1)
            sgn = (2 * sgn - 1).astype(jnp.float32)
            value = summed[:, q * BLOCK : (q + 2) * BLOCK] * sgn
            high = value.astype(jnp.bfloat16)
            rest = value - high.astype(jnp.float32)
            mid = rest.astype(jnp.bfloat16)
            low = (rest - mid.astype(jnp.float32)).astype(jnp.bfloat16)
            h = h_two[...]
            turned = (
                jnp.dot(low, h, preferred_element_type=jnp.float32)
                + jnp.dot(mid, h, preferred_element_type=jnp.float32)
                + jnp.dot(high, h, preferred_element_type=jnp.float32)
            ) * norm_h
            for r in (0, 1):
                k = j * blocks + q + r
                column = jnp.broadcast_to(e[:, k : k + 1], (tok, BLOCK))
                scaled = turned[:, r * BLOCK : (r + 1) * BLOCK] * power_table(column, -1)
                coded = jnp.clip(scaled, -clip_level, clip_level).astype(jnp.bfloat16)
                ys[j, :, (q + r) * BLOCK : (q + r + 1) * BLOCK] = (
                    coded.astype(jnp.float32) * power_table(column, 1)
                ).astype(jnp.bfloat16)

        @pl.when(s < n_sec - 1)
        def _():
            for z_hi in (0, 1):
                hand(j, z_hi).start()

    def fold_weights(j):
        def body(i, carry):
            b = (i // blocks) * (own // BLOCK) + j * blocks + i % blocks
            scale = (2 * row(signs, b) - 1).astype(jnp.float32) * row(gain, b)
            turn = h_one[...] * scale
            high = turn.astype(jnp.bfloat16)
            low = (turn - high.astype(jnp.float32)).astype(jnp.bfloat16)
            rows = pl.ds(pl.multiple_of(b * BLOCK, BLOCK), BLOCK)
            w = jnp.concatenate([wv[0, rows, :], wv[1, rows, :]], axis=1)
            prod = jnp.dot(
                jnp.concatenate([high, low], axis=1),
                jnp.concatenate([w, w], axis=0),
                preferred_element_type=jnp.float32,
            )
            wp[rows, :] = (prod * norm_h).astype(jnp.bfloat16)
            return carry

        lax.fori_loop(0, 2 * NX * blocks, body, 0, unroll=2)

    def spread(j):
        @pl.when(s > 0)
        def _():
            for z_hi in (0, 1):
                remote(ys.at[j], g.at[x, j, z_hi], y_s.at[z_hi, j], y_r.at[z_hi, j], right).wait_recv()

        for d, z_hi in ((0, 0), (1, 1), (0, 1), (1, 0)):
            gather(j, d, z_hi).start()

    def pass_on(j):
        for d in (0, 1):
            got_gather(j, d, d)
            forward(j, d).start()

    def project(j, col, z_hi):
        v = g[col, j, z_hi]
        rows = pl.ds(pl.multiple_of((z_hi * NX + col) * own + j * width, width), width)
        acc[...] += jnp.dot(v, wp[rows, :], preferred_element_type=jnp.float32)
        f = v.astype(jnp.float32)
        sq = f * f
        total = sq[:, :BLOCK]
        for q in range(1, blocks):
            total = total + sq[:, q * BLOCK : (q + 1) * BLOCK]
        ssq[...] += total

    for k in range(slices):
        combine(k)
        if k + 1 < slices:
            for d in (0, 1):
                near(k + 1, d).start()
        if k + 2 < slices:
            for d in (0, 1):
                far(k + 2, d).start()
        if k == 0:
            for c in small:
                c.wait()
        fold_weights(k)
        if k >= 1:
            exchange(k - 1)
        if k >= 3:
            encode(k - 3)

    spread(0)
    spread(1)
    exchange(slices - 1)
    for k in range(slices):
        if k < 3:
            encode(slices - 3 + k)
        if k + 2 < slices:
            spread(k + 2)
        pass_on(k)
        project(k, x, 0)
        project(k, x, 1)
        project(k, xl, 0)
        project(k, xr, 1)
        got_gather(k, 0, 1)
        project(k, xl, 1)
        got_gather(k, 1, 0)
        project(k, xr, 0)
        if k >= 1:
            for d in (0, 1):
                got_forward(k - 1, d)
                project(k - 1, xo, d)
        for d in (0, 1):
            far(k, d).wait_send()
            near(k, d).wait_send()
            comb(k, d).wait_send()
        if k >= 1:
            pair(k - 1).wait_send()
            for d in (0, 1):
                forward(k - 1, d).wait_send()
                for z_hi in (0, 1):
                    gather(k - 1, d, z_hi).wait_send()
        if k == slices - 1:
            pair(k).wait_send()

            @pl.when(s < n_sec - 1)
            def _():
                for j in range(slices):
                    for z_hi in (0, 1):
                        hand(j, z_hi).wait_send()

    last = slices - 1
    for d in (0, 1):
        got_forward(last, d)
        project(last, xo, d)
    mean = jnp.sum(ssq[...], axis=1, keepdims=True) * jnp.float32(1.0 / (2 * NX * own))
    result = acc[...] * lax.rsqrt(mean + norm_eps)
    out[0, 0] = result[:, :BLOCK].astype(out.dtype)
    out[0, 1] = result[:, BLOCK:].astype(out.dtype)
    for d in (0, 1):
        forward(last, d).wait_send()
        for z_hi in (0, 1):
            gather(last, d, z_hi).wait_send()


def on_device(partials, residual, exponents, signs, gain, kv_weight):
    tok, own = residual.shape[1], residual.shape[2]
    model = signs.shape[0]
    c = SLICES
    width = own // c
    bf, f32 = jnp.bfloat16, jnp.float32
    dma = pltpu.SemaphoreType.DMA
    blocks2d = (model // BLOCK, BLOCK)
    return pl.pallas_call(
        kernel,
        out_shape=jax.ShapeDtypeStruct((1, 2, tok, kv_weight.shape[3]), bf),
        in_specs=[pl.BlockSpec(memory_space=pl.ANY)] * 6,
        out_specs=pl.BlockSpec(memory_space=pltpu.VMEM),
        scratch_shapes=[
            pltpu.VMEM((4, c, tok, width), bf),
            pltpu.VMEM((2, c, tok, width), bf),
            pltpu.VMEM((2, 2, c, tok, width), bf),
            pltpu.VMEM((c, tok, width), bf),
            pltpu.VMEM((c, tok, width), bf),
            pltpu.VMEM((c, tok, width), bf),
            pltpu.VMEM((NX, c, 2, tok, width), bf),
            pltpu.VMEM((2, model, BLOCK), bf),
            pltpu.VMEM((model, 2 * BLOCK), bf),
            pltpu.VMEM((tok, own), bf),
            pltpu.VMEM((tok, own // BLOCK), jnp.int32),
            pltpu.VMEM(blocks2d, jnp.int32),
            pltpu.VMEM(blocks2d, f32),
            pltpu.VMEM((BLOCK, BLOCK), f32),
            pltpu.VMEM((2 * BLOCK, 2 * BLOCK), bf),
            pltpu.VMEM((tok, 2 * BLOCK), f32),
            pltpu.VMEM((tok, BLOCK), f32),
            dma((4, c)),
            dma((6,)),
            dma((2, c)),
            dma((2, c)),
            dma((2, c)),
            dma((2, c)),
            dma((2, 2, c)),
            dma((c,)),
            dma((c,)),
            dma((2, c)),
            dma((2, c)),
            dma((2, 2, c)),
            dma((2, 2, c)),
            dma((2, c)),
            dma((2, c)),
        ],
        compiler_params=pltpu.CompilerParams(
            collective_id=0, has_side_effects=True, vmem_limit_bytes=48 << 20
        ),
        cost_estimate=pl.CostEstimate(
            flops=6 * tok * model * 2 * BLOCK, bytes_accessed=14 << 20, transcendentals=tok
        ),
        name="relay",
    )(partials, residual, exponents, signs.reshape(blocks2d), gain.reshape(blocks2d), kv_weight)


def solution(mesh):
    placed = (
        P("section", "tensor", "dp", None),
        P("section", "dp", "tensor"),
        P("section", "dp", "tensor"),
        P(),
        P(),
        P("section", None, None, "tensor"),
    )
    return jax.shard_map(
        on_device,
        mesh=mesh,
        in_specs=placed,
        out_specs=P("section", None, "dp", "tensor"),
        check_vma=False,
    )
```

time: 304 us -> 116 us (0.38)
  waiting for transfers between devices: 202 us -> 0 us
  Pallas kernels: 0 us -> 107 us
  blocking collectives: 39.9 us -> 0 us
  matrix products: 19.3 us -> 0 us
  between operations: 13.5 us -> 0.02 us
  local copies, waits for them, and re-layouts: 15.2 us -> 6.33 us
  starting transfers between devices: 5.36 us -> 0 us
  other arithmetic: 4.86 us -> 0 us
    reduce_scatter x1 -> x0, waiting for transfers between devices: 131 us -> none  [on_device(): lax.psum_scatter(partials[0, 0].astype(jnp.float32).astype(jnp.bfloat16),...]
    pallas_call x0 -> x1, Pallas kernels: none -> 107 us  [on_device(): pl.pallas_call(kernel, out_shape=jax.ShapeDtypeStruct((1, 2, tok, kv_weig...]
    all_gather x1 -> x0, waiting for transfers between devices: 52.2 us -> none  [on_device(): lax.all_gather(got_coded, 'tensor', axis=1, tiled=True)]
    all_gather x1 -> x0, blocking collectives: 39.9 us -> none  [on_device(): lax.all_gather(got_expo, 'tensor', axis=1, tiled=True)]
    dot_general x3 -> x0, matrix products: 19.3 us -> none  [the longest x1 10.1 us: decode(): jnp.einsum('tbk,kj->tbj', shaped, matrix_h, precision=lax.Precision.HIGHEST)]
    ppermute x2 -> x0, waiting for transfers between devices: 18.4 us -> none  [shifted(): return lax.ppermute(x, axis, pairs)]
    convert_element_type x1 -> x0, local copies, waits for them, and re-layouts: 7.35 us -> none  [normalize(): return (decoded * lax.rsqrt(meansq + norm_eps) * gain).astype(jnp.bfloat16)]
    reshape x1 -> x0, local copies, waits for them, and re-layouts: 6.94 us -> none  [decode(): coded.astype(jnp.float32).reshape(rows_n, cols_n // blk, blk)]
  transfers between devices with their start and end apart: 4 -> 0, of which waited for: 4 -> 0; matrix products, arithmetic and copies ran while one was open for 1% -> 0% of each run, Pallas kernels for 0% -> 0%
where the time goes in v1:
time: 116 us; the launch traced here: 114 us
  Pallas kernels  107 us (92%)
  local copies, waits for them, and re-layouts  6.33 us (5%)
    pallas_call x1, Pallas kernels, on_device(): pl.pallas_call(kernel, out_shape=jax.ShapeDtypeStruct((1, 2, tok, kv_weig...  107 us
    unnamed x10, local copies, waits for them, and re-layouts  6.33 us

profile of v1, /device:TPU:34, one launch (start us, length us, event | category | flops | bytes accessed | tf_op | source)
XLA Modules:
  0.0 113.8 jit_solution(3902082051753874606)
XLA Ops:
  0.0 0.8 copy.7.expo_h
  0.8 0.0 copy-start
  0.8 2.2 %copy-done = bf16[1,1,128,16384]{3,2,1,0:T(8,128)(2,1)S(1)} copy-done((bf16[1,1,128,16384]{3,2,1,0:T(8,128)(2,1)S(1)}, bf16[1,1,128,16384]{3,2,1,0:T(8,128)(2,1)}, u32[]{:S(2)}) %copy-start) | copy-done | bytes 4194328
  3.0 0.0 copy-start.1
  3.0 1.0 copy-done.1
  4.0 0.0 copy-start.2
  4.0 0.8 copy-done.2
  4.9 0.0 copy-start.3
  4.9 0.8 copy-done.3
  5.7 107.5 %relay.1 = bf16[1,2,128,128]{3,2,1,0:T(8,128)(2,1)S(1)} custom-call(bf16[1,1,128,16384]{3,2,1,0:T(8,128)(2,1)S(1)} %copy-done, bf16[1,128,2048]{2,1,0:T(8,128)(2,1)S(1)} %copy-done.1, s32[1,128,16]{2,1,0:T(8,128)S(1)} %copy.7.expo_h, s32[128,128]{1,0:T(8,128)S(1)} %bitcast.2, f32[128,128]{1,0:T(8,128)S(1)} %bitcast.3, bf16[1,2,16384,128]{3,2,1,0:T(8,128)(2,1)} %w_h.1), custom_call_target="tpu_custom_call" | custom-call | flops 3221225472 | bytes 14680064 | tf_op jit(solution)/shard_map/relay/pallas_call | solution.py:352
  113.2 0.6 copy.9
Async XLA Ops:
  0.8 2.2 %copy-start = (bf16[1,1,128,16384]{3,2,1,0:T(8,128)(2,1)S(1)}, bf16[1,1,128,16384]{3,2,1,0:T(8,128)(2,1)}, u32[]{:S(2)}) copy-start(bf16[1,1,128,16384]{3,2,1,0:T(8,128)(2,1)} %part.1) | copy-start | bytes 12582916
  3.0 1.0 copy-start.1
  4.0 0.8 copy-start.2
  4.9 0.8 copy-start.3

commit v2 on v1

--- a/solution.py
+++ b/solution.py
@@ -15,6 +15,14 @@
 exp_high = -3
 norm_eps = 1e-05
 SLICES = 8
+TAIL = (
+    "S0", "S1", "X7", "S2", "E5", "P0", "S3", "E6", "R0", "R1", "P1", "S4", "E7", "R2",
+    "P2", "R3", "S5", "P3", "R4", "N0", "S6", "P4", "N1", "R5", "S7", "P5", "R6", "N2",
+    "R7", "P6", "N3", "O0", "P7", "N4", "F0", "F1", "O1", "N5", "F2", "F3", "O2", "N6",
+    "F4", "Q0", "N7", "F5", "O3", "Q1", "F6", "F7", "M0", "O4", "Q2", "M1", "G0", "O5",
+    "Q3", "M2", "G1", "O6", "Q4", "M3", "G2", "O7", "Q5", "M4", "G3", "Q6", "M5", "G4",
+    "Q7", "M6", "G5", "M7", "G6", "G7",
+)
 NX = 4
 
 
@@ -43,7 +51,7 @@
 def kernel(
     part, resid, expo_h, signs_h, gain_h, w_h, out,
     pv, ab, rsb, zs, zr, ys, g, wv, wp, rv, expo, signs, gain, h_one, h_two, acc, ssq,
-    pv_s, in_s, a_s, a_r, raw_s, comb_s, rs_r, z_s, z_r, y_s, y_r, ag_s, ag_r, fw_s, fw_r,
+    pv_s, in_s, a_s, a_r, raw_s, comb_s, rs_r, z_s, z_r, y_s, y_r, c_s, ag_s, ag_r, fw_s, fw_r,
 ):
     n_sec = lax.axis_size("section")
     s, dp, t = lax.axis_index("section"), lax.axis_index("dp"), lax.axis_index("tensor")
@@ -93,17 +101,15 @@
 
     @pl.when(s > 0)
     def _():
-        greet(at(s - 1, 0, x))
-        greet(at(s - 1, 1, x))
+        greet(at(s - 1, zh, x))
 
     @pl.when(s < n_sec - 1)
     def _():
-        greet(at(s + 1, 0, x))
-        greet(at(s + 1, 1, x))
+        greet(at(s + 1, zh, x))
 
     before = (s + n_sec - 1) // n_sec
     after = (2 * n_sec - 2 - s) // n_sec
-    pl.semaphore_wait(bar, 3 + 2 * before + 2 * after)
+    pl.semaphore_wait(bar, 3 + before + after)
 
     def remote(src, dst, send, recv, device):
         return pltpu.make_async_remote_copy(
@@ -127,25 +133,30 @@
     def pair(j):
         return remote(zs.at[j], zr.at[j], z_s.at[j], z_r.at[j], across)
 
-    def hand(j, z_hi):
-        return remote(
-            ys.at[j], g.at[x, j, zh], y_s.at[z_hi, j], y_r.at[zh, j], at(s + 1, z_hi, x)
-        )
+    def hand(j):
+        return remote(ys.at[j], g.at[x, j, zh], y_s.at[j], y_r.at[zh, j], at(s + 1, zh, x))
+
+    def relay_across(j):
+        return remote(g.at[x, j, zh], g.at[x, j, zh], c_s.at[j], y_r.at[zh, j], across)
 
     def gather(j, d, z_hi):
         device = right if d == 0 else left
         return remote(g.at[x, j, z_hi], g.at[x, j, z_hi], ag_s.at[d, z_hi, j], ag_r.at[d, z_hi, j], device)
 
-    def forward(j, d):
-        device, col = (right, xl) if d == 0 else (left, xr)
-        return remote(g.at[col, j, d], g.at[col, j, d], fw_s.at[d, j], fw_r.at[d, j], device)
+    def onward(j, z_hi):
+        d = (z_hi + j) % 2
+        return d, (x + 3 + 2 * d) % NX, at(s, zh, (x + 1 + 2 * d) % NX)
+
+    def forward(j, z_hi):
+        d, col, device = onward(j, z_hi)
+        return remote(g.at[col, j, z_hi], g.at[col, j, z_hi], fw_s.at[z_hi, j], fw_r.at[z_hi, j], device)
 
     def got_gather(j, d, z_hi):
-        col = xl if d == 0 else xr
+        col = (x + 3 + 2 * d) % NX
         remote(g.at[col, j, z_hi], g.at[col, j, z_hi], ag_s.at[d, z_hi, j], ag_r.at[d, z_hi, j], right).wait_recv()
 
-    def got_forward(j, d):
-        remote(g.at[xo, j, d], g.at[xo, j, d], fw_s.at[d, j], fw_r.at[d, j], right).wait_recv()
+    def got_forward(j, z_hi):
+        remote(g.at[xo, j, z_hi], g.at[xo, j, z_hi], fw_s.at[z_hi, j], fw_r.at[z_hi, j], right).wait_recv()
 
     for d in (0, 1):
         far(0, d).start()
@@ -196,7 +207,7 @@
             + zr[j].astype(jnp.float32)
             + rv[:, j * width : (j + 1) * width].astype(jnp.float32)
         )
-        e = expo[...]
+        e = jnp.swapaxes(expo[...], 0, 1)
         for q in range(0, blocks, 2):
             b = t * (own // BLOCK) + j * blocks + q
             sgn = jnp.concatenate([row(signs, b), row(signs, b + 1)], axis=1)
@@ -223,8 +234,7 @@
 
         @pl.when(s < n_sec - 1)
         def _():
-            for z_hi in (0, 1):
-                hand(j, z_hi).start()
+            hand(j).start()
 
     def fold_weights(j):
         def body(i, carry):
@@ -245,19 +255,34 @@
 
         lax.fori_loop(0, 2 * NX * blocks, body, 0, unroll=2)
 
+    def arrived(j, z_hi):
+        remote(g.at[x, j, z_hi], g.at[x, j, z_hi], c_s.at[j], y_r.at[z_hi, j], right).wait_recv()
+
+    def relay(j):
+        @pl.when(s > 0)
+        def _():
+            relay_across(j).start()
+
     def spread(j):
         @pl.when(s > 0)
         def _():
-            for z_hi in (0, 1):
-                remote(ys.at[j], g.at[x, j, z_hi], y_s.at[z_hi, j], y_r.at[z_hi, j], right).wait_recv()
-
-        for d, z_hi in ((0, 0), (1, 1), (0, 1), (1, 0)):
-            gather(j, d, z_hi).start()
-
-    def pass_on(j):
-        for d in (0, 1):
-            got_gather(j, d, d)
-            forward(j, d).start()
+            arrived(j, zh)
+
+        for d in (0, 1):
+            gather(j, d, zh).start()
+
+    def spread_other(j):
+        @pl.when(s > 0)
+        def _():
+            arrived(j, 1 - zh)
+
+        for d in (0, 1):
+            gather(j, d, 1 - zh).start()
+
+    def pass_on(j, z_hi):
+        d, _, _ = onward(j, z_hi)
+        got_gather(j, d, z_hi)
+        forward(j, z_hi).start()
 
     def project(j, col, z_hi):
         v = g[col, j, z_hi]
@@ -270,14 +295,40 @@
             total = total + sq[:, q * BLOCK : (q + 1) * BLOCK]
         ssq[...] += total
 
+    def send_on(j):
+        if j < slices:
+            for d in (0, 1):
+                near(j, d).start()
+        if j + 1 < slices:
+            for d in (0, 1):
+                far(j + 1, d).start()
+
+    def project_near(j, z_hi):
+        d, col, _ = onward(j, z_hi)
+        project(j, x, z_hi)
+        project(j, col, z_hi)
+        got_gather(j, 1 - d, z_hi)
+        project(j, (x + 1 + 2 * d) % NX, z_hi)
+
+    def project_far(j, z_hi):
+        got_forward(j, z_hi)
+        project(j, xo, z_hi)
+
+    def sent_sums(k):
+        for d in (0, 1):
+            far(k, d).wait_send()
+            near(k, d).wait_send()
+            comb(k, d).wait_send()
+        pair(k).wait_send()
+
+    def sent_gather(j, z_hi):
+        forward(j, z_hi).wait_send()
+        for d in (0, 1):
+            gather(j, d, z_hi).wait_send()
+
     for k in range(slices):
         combine(k)
-        if k + 1 < slices:
-            for d in (0, 1):
-                near(k + 1, d).start()
-        if k + 2 < slices:
-            for d in (0, 1):
-                far(k + 2, d).start()
+        send_on(k + 1)
         if k == 0:
             for c in small:
                 c.wait()
@@ -287,58 +338,43 @@
         if k >= 3:
             encode(k - 3)
 
-    spread(0)
-    spread(1)
-    exchange(slices - 1)
-    for k in range(slices):
-        if k < 3:
-            encode(slices - 3 + k)
-        if k + 2 < slices:
-            spread(k + 2)
-        pass_on(k)
-        project(k, x, 0)
-        project(k, x, 1)
-        project(k, xl, 0)
-        project(k, xr, 1)
-        got_gather(k, 0, 1)
-        project(k, xl, 1)
-        got_gather(k, 1, 0)
-        project(k, xr, 0)
-        if k >= 1:
-            for d in (0, 1):
-                got_forward(k - 1, d)
-                project(k - 1, xo, d)
-        for d in (0, 1):
-            far(k, d).wait_send()
-            near(k, d).wait_send()
-            comb(k, d).wait_send()
-        if k >= 1:
-            pair(k - 1).wait_send()
-            for d in (0, 1):
-                forward(k - 1, d).wait_send()
-                for z_hi in (0, 1):
-                    gather(k - 1, d, z_hi).wait_send()
-        if k == slices - 1:
-            pair(k).wait_send()
-
-            @pl.when(s < n_sec - 1)
-            def _():
-                for j in range(slices):
-                    for z_hi in (0, 1):
-                        hand(j, z_hi).wait_send()
-
-    last = slices - 1
-    for d in (0, 1):
-        got_forward(last, d)
-        project(last, xo, d)
+    for step in TAIL:
+        kind, k = step[0], int(step[1:])
+        if kind == "X":
+            exchange(k)
+        elif kind == "E":
+            encode(k)
+        elif kind == "R":
+            relay(k)
+        elif kind == "S":
+            spread(k)
+        elif kind == "O":
+            spread_other(k)
+        elif kind in "PQ":
+            pass_on(k, zh if kind == "P" else 1 - zh)
+        elif kind in "NM":
+            project_near(k, zh if kind == "N" else 1 - zh)
+            if kind == "N":
+                sent_sums(k)
+        elif kind in "FG":
+            z_hi = zh if kind == "F" else 1 - zh
+            project_far(k, z_hi)
+            sent_gather(k, z_hi)
+
+    @pl.when(s < n_sec - 1)
+    def _():
+        for j in range(slices):
+            hand(j).wait_send()
+
+    @pl.when(s > 0)
+    def _():
+        for j in range(slices):
+            relay_across(j).wait_send()
+
     mean = jnp.sum(ssq[...], axis=1, keepdims=True) * jnp.float32(1.0 / (2 * NX * own))
     result = acc[...] * lax.rsqrt(mean + norm_eps)
     out[0, 0] = result[:, :BLOCK].astype(out.dtype)
     out[0, 1] = result[:, BLOCK:].astype(out.dtype)
-    for d in (0, 1):
-        forward(last, d).wait_send()
-        for z_hi in (0, 1):
-            gather(last, d, z_hi).wait_send()
 
 
 def on_device(partials, residual, exponents, signs, gain, kv_weight):
@@ -365,7 +401,7 @@
             pltpu.VMEM((2, model, BLOCK), bf),
             pltpu.VMEM((model, 2 * BLOCK), bf),
             pltpu.VMEM((tok, own), bf),
-            pltpu.VMEM((tok, own // BLOCK), jnp.int32),
+            pltpu.VMEM((own // BLOCK, tok), jnp.int32),
             pltpu.VMEM(blocks2d, jnp.int32),
             pltpu.VMEM(blocks2d, f32),
             pltpu.VMEM((BLOCK, BLOCK), f32),
@@ -381,21 +417,22 @@
             dma((2, 2, c)),
             dma((c,)),
             dma((c,)),
-            dma((2, c)),
-            dma((2, c)),
+            dma((c,)),
+            dma((2, c)),
+            dma((c,)),
             dma((2, 2, c)),
             dma((2, 2, c)),
             dma((2, c)),
             dma((2, c)),
         ],
         compiler_params=pltpu.CompilerParams(
-            collective_id=0, has_side_effects=True, vmem_limit_bytes=48 << 20
+            collective_id=0, has_side_effects=True, vmem_limit_bytes=62 << 20
         ),
         cost_estimate=pl.CostEstimate(
             flops=6 * tok * model * 2 * BLOCK, bytes_accessed=14 << 20, transcendentals=tok
         ),
         name="relay",
-    )(partials, residual, exponents, signs.reshape(blocks2d), gain.reshape(blocks2d), kv_weight)
+    )(partials, residual, jnp.swapaxes(exponents, 1, 2), signs.reshape(blocks2d), gain.reshape(blocks2d), kv_weight)
 
 
 def solution(mesh):

time: 116 us -> 92.8 us (0.80); the launches traced: 114 us -> 92.2 us
  Pallas kernels: 107 us -> 90.7 us
  local copies, waits for them, and re-layouts: 6.33 us -> 1.47 us
    pallas_call x1, Pallas kernels: 107 us -> 90.7 us  [on_device(): pl.pallas_call(kernel, out_shape=jax.ShapeDtypeStruct((1, 2, tok, kv_weig...]
    unnamed x10 -> x1, local copies, waits for them, and re-layouts: 6.33 us -> 1.47 us
where the time goes in v2:
time: 92.8 us; the launch traced here: 92.2 us
  Pallas kernels  90.7 us (98%)
  local copies, waits for them, and re-layouts  1.47 us (2%)
    pallas_call x1, Pallas kernels, on_device(): pl.pallas_call(kernel, out_shape=jax.ShapeDtypeStruct((1, 2, tok, kv_weig...  90.7 us

profile of v2, /device:TPU:34, one launch (start us, length us, event | category | flops | bytes accessed | tf_op | source)
XLA Modules:
  0.0 92.2 jit_solution(17910329676153298193)
XLA Ops:
  0.0 90.7 %relay.1 = bf16[1,2,128,128]{3,2,1,0:T(8,128)(2,1)} custom-call(bf16[1,1,128,16384]{3,2,1,0:T(8,128)(2,1)} %part.1, bf16[1,128,2048]{2,1,0:T(8,128)(2,1)} %resid.1, s32[1,16,128]{2,1,0:T(8,128)} %bitcast.5, s32[128,128]{1,0:T(8,128)} %bitcast.3, f32[128,128]{1,0:T(8,128)} %bitcast.4, bf16[1,2,16384,128]{3,2,1,0:T(8,128)(2,1)} %w_h.1), custom_call_target="tpu_custom_call" | custom-call | flops 3221225472 | bytes 14680064 | tf_op jit(solution)/shard_map/relay/pallas_call | solution.py:388
  90.8 1.5 %copy.8 = bf16[1,2,128,128]{3,2,1,0:T(8,128)(2,1)} copy(bf16[1,2,128,128]{3,2,1,0:T(8,128)(2,1)} %relay.1) | data formatting | bytes 131072

commit v3 on v2

--- a/solution.py
+++ b/solution.py
@@ -16,14 +16,15 @@
 norm_eps = 1e-05
 SLICES = 8
 TAIL = (
-    "S0", "S1", "X7", "S2", "E5", "P0", "S3", "E6", "R0", "R1", "P1", "S4", "E7", "R2",
-    "P2", "R3", "S5", "P3", "R4", "N0", "S6", "P4", "N1", "R5", "S7", "P5", "R6", "N2",
-    "R7", "P6", "N3", "O0", "P7", "N4", "F0", "F1", "O1", "N5", "F2", "F3", "O2", "N6",
-    "F4", "Q0", "N7", "F5", "O3", "Q1", "F6", "F7", "M0", "O4", "Q2", "M1", "G0", "O5",
-    "Q3", "M2", "G1", "O6", "Q4", "M3", "G2", "O7", "Q5", "M4", "G3", "Q6", "M5", "G4",
-    "Q7", "M6", "G5", "M7", "G6", "G7",
+    "S2", "D3", "S3", "X7", "E5", "P0", "P1", "E6", "S4", "R0", "P2", "D5", "S5", "R1",
+    "E7", "P3", "S6", "R2", "N0", "P4", "D7", "S7", "R3", "N1", "P5", "R4", "N2", "R5",
+    "P6", "N3", "R6", "O0", "P7", "R7", "N4", "F0", "F1", "O1", "N5", "F2", "F3", "O2",
+    "N6", "F4", "Q0", "N7", "F5", "O3", "Q1", "F6", "F7", "M0", "O4", "Q2", "M1", "G0",
+    "O5", "Q3", "M2", "G1", "O6", "Q4", "M3", "G2", "O7", "Q5", "M4", "G3", "Q6", "M5",
+    "G4", "Q7", "M6", "G5", "M7", "G6", "G7",
 )
 NX = 4
+NY = 4
 
 
 def power_table(exponents_in, direction):
@@ -50,8 +51,8 @@
 
 def kernel(
     part, resid, expo_h, signs_h, gain_h, w_h, out,
-    pv, ab, rsb, zs, zr, ys, g, wv, wp, rv, expo, signs, gain, h_one, h_two, acc, ssq,
-    pv_s, in_s, a_s, a_r, raw_s, comb_s, rs_r, z_s, z_r, y_s, y_r, c_s, ag_s, ag_r, fw_s, fw_r,
+    pv, ab, rsb, zs, zr, ys, rb, g, wv, wp, rv, expo, signs, gain, h_one, h_two, acc, ssq,
+    pv_s, in_s, a_s, a_r, raw_s, comb_s, rs_r, z_s, z_r, y_s, y_r, c_s, d_s, d_r, ag_s, ag_r, fw_s, fw_r,
 ):
     n_sec = lax.axis_size("section")
     s, dp, t = lax.axis_index("section"), lax.axis_index("dp"), lax.axis_index("tensor")
@@ -60,6 +61,10 @@
     tok, slices, width = pv.shape[2], pv.shape[1], pv.shape[3]
     own = slices * width
     blocks = width // BLOCK
+    closing = (s % NY) // (NY - 1) * ((2 * n_sec - 2 - s) // n_sec)
+    first = 1 - (s % NY + NY - 1) // NY
+    between = first * (1 - s // (n_sec - NY))
+    opening = first * ((s + n_sec - 1) // n_sec)
     norm_h = jnp.float32(1.0 / math.sqrt(BLOCK))
 
     def at(section, z_hi, col):
@@ -84,32 +89,40 @@
         pltpu.make_async_copy(w_h.at[0, 0], wv.at[0], in_s.at[4]),
         pltpu.make_async_copy(w_h.at[0, 1], wv.at[1], in_s.at[5]),
     ]
+    bar = pltpu.get_barrier_semaphore()
+
+    def greet(device):
+        pl.semaphore_signal(bar, inc=1, device_id=device, device_id_type=MESH)
+
+    for device in (right, left, across):
+        greet(device)
+
+    @pl.when(s > 0)
+    def _():
+        greet(at(s - 1, zh, x))
+
+    @pl.when(s < n_sec - 1)
+    def _():
+        greet(at(s + 1, zh, x))
+
+    @pl.when(closing == 1)
+    def _():
+        greet(at(s - (NY - 1), zh, x))
+
+    @pl.when(between == 1)
+    def _():
+        greet(at(s + NY - 1, zh, x))
+        greet(at(s + NY, zh, x))
+
+    @pl.when(opening == 1)
+    def _():
+        greet(at(s - NY, zh, x))
+
+    before = (s + n_sec - 1) // n_sec
+    after = (2 * n_sec - 2 - s) // n_sec
     for c in own_loads[:8]:
         c.start()
-    for c in small:
-        c.start()
-    for c in own_loads[8:]:
-        c.start()
-
-    bar = pltpu.get_barrier_semaphore()
-
-    def greet(device):
-        pl.semaphore_signal(bar, inc=1, device_id=device, device_id_type=MESH)
-
-    for device in (right, left, across):
-        greet(device)
-
-    @pl.when(s > 0)
-    def _():
-        greet(at(s - 1, zh, x))
-
-    @pl.when(s < n_sec - 1)
-    def _():
-        greet(at(s + 1, zh, x))
-
-    before = (s + n_sec - 1) // n_sec
-    after = (2 * n_sec - 2 - s) // n_sec
-    pl.semaphore_wait(bar, 3 + before + after)
+    pl.semaphore_wait(bar, 3 + before + after + closing + 2 * between + opening)
 
     def remote(src, dst, send, recv, device):
         return pltpu.make_async_remote_copy(
@@ -135,6 +148,12 @@
 
     def hand(j):
         return remote(ys.at[j], g.at[x, j, zh], y_s.at[j], y_r.at[zh, j], at(s + 1, zh, x))
+
+    def detour(j):
+        return remote(ys.at[j], rb.at[j // 2], y_s.at[j], d_r.at[j // 2], at(s - (NY - 1), zh, x))
+
+    def detour_on(j):
+        return remote(rb.at[j // 2], g.at[x, j, zh], d_s.at[j // 2], y_r.at[zh, j], at(s + NY, zh, x))
 
     def relay_across(j):
         return remote(g.at[x, j, zh], g.at[x, j, zh], c_s.at[j], y_r.at[zh, j], across)
@@ -164,6 +183,10 @@
         near(0, d).start()
     for d in (0, 1):
         far(1, d).start()
+    for c in small:
+        c.start()
+    for c in own_loads[8:]:
+        c.start()
 
     h_one[...] = hadamard_signs(BLOCK, BLOCK)
     h_two[...] = hadamard_signs(2 * BLOCK, 2 * BLOCK).astype(jnp.bfloat16)
@@ -232,9 +255,27 @@
                     coded.astype(jnp.float32) * power_table(column, 1)
                 ).astype(jnp.bfloat16)
 
-        @pl.when(s < n_sec - 1)
+        if j % 2 == 0:
+
+            @pl.when(s < n_sec - 1)
+            def _():
+                hand(j).start()
+
+        else:
+
+            @pl.when((s < n_sec - 1) & (closing == 0))
+            def _():
+                hand(j).start()
+
+            @pl.when(closing == 1)
+            def _():
+                detour(j).start()
+
+    def step_aside(j):
+        @pl.when(between == 1)
         def _():
-            hand(j).start()
+            remote(rb.at[j // 2], rb.at[j // 2], d_s.at[j // 2], d_r.at[j // 2], right).wait_recv()
+            detour_on(j).start()
 
     def fold_weights(j):
         def body(i, carry):
@@ -329,14 +370,19 @@
     for k in range(slices):
         combine(k)
         send_on(k + 1)
+        if k == slices - 1:
+            spread(0)
+            spread(1)
         if k == 0:
             for c in small:
                 c.wait()
-        fold_weights(k)
         if k >= 1:
             exchange(k - 1)
         if k >= 3:
             encode(k - 3)
+        if k == 6:
+            step_aside(1)
+        fold_weights(k)
 
     for step in TAIL:
         kind, k = step[0], int(step[1:])
@@ -344,6 +390,8 @@
             exchange(k)
         elif kind == "E":
             encode(k)
+        elif kind == "D":
+            step_aside(k)
         elif kind == "R":
             relay(k)
         elif kind == "S":
@@ -370,6 +418,11 @@
     def _():
         for j in range(slices):
             relay_across(j).wait_send()
+
+    @pl.when(between == 1)
+    def _():
+        for j in range(1, slices, 2):
+            detour_on(j).wait_send()
 
     mean = jnp.sum(ssq[...], axis=1, keepdims=True) * jnp.float32(1.0 / (2 * NX * own))
     result = acc[...] * lax.rsqrt(mean + norm_eps)
@@ -397,6 +450,7 @@
             pltpu.VMEM((c, tok, width), bf),
             pltpu.VMEM((c, tok, width), bf),
             pltpu.VMEM((c, tok, width), bf),
+            pltpu.VMEM((c // 2, tok, width), bf),
             pltpu.VMEM((NX, c, 2, tok, width), bf),
             pltpu.VMEM((2, model, BLOCK), bf),
             pltpu.VMEM((model, 2 * BLOCK), bf),
@@ -420,6 +474,8 @@
             dma((c,)),
             dma((2, c)),
             dma((c,)),
+            dma((c // 2,)),
+            dma((c // 2,)),
             dma((2, 2, c)),
             dma((2, 2, c)),
             dma((2, c)),

time: 92.8 us -> 91.1 us (0.982)
  Pallas kernels: 90.7 us -> 89.5 us
    pallas_call x1, Pallas kernels: 90.7 us -> 89.5 us  [on_device(): pl.pallas_call(kernel, out_shape=jax.ShapeDtypeStruct((1, 2, tok, kv_weig...]
where the time goes in v3:
time: 91.1 us; the launch traced here: 90.9 us
  Pallas kernels  89.5 us (98%)
  local copies, waits for them, and re-layouts  1.47 us (2%)
    pallas_call x1, Pallas kernels, on_device(): pl.pallas_call(kernel, out_shape=jax.ShapeDtypeStruct((1, 2, tok, kv_weig...  89.5 us

profile of v3, /device:TPU:34, one launch (start us, length us, event | category | flops | bytes accessed | tf_op | source)
XLA Modules:
  0.0 90.9 jit_solution(13715636309126440919)
XLA Ops:
  0.0 89.5 %relay.1 = bf16[1,2,128,128]{3,2,1,0:T(8,128)(2,1)} custom-call(bf16[1,1,128,16384]{3,2,1,0:T(8,128)(2,1)} %part.1, bf16[1,128,2048]{2,1,0:T(8,128)(2,1)} %resid.1, s32[1,16,128]{2,1,0:T(8,128)} %bitcast.5, s32[128,128]{1,0:T(8,128)} %bitcast.3, f32[128,128]{1,0:T(8,128)} %bitcast.4, bf16[1,2,16384,128]{3,2,1,0:T(8,128)(2,1)} %w_h.1), custom_call_target="tpu_custom_call" | custom-call | flops 3221225472 | bytes 14680064 | tf_op jit(solution)/shard_map/relay/pallas_call | solution.py:441
  89.5 1.5 %copy.8 = bf16[1,2,128,128]{3,2,1,0:T(8,128)(2,1)} copy(bf16[1,2,128,128]{3,2,1,0:T(8,128)(2,1)} %relay.1) | data formatting | bytes 131072

commit v4 on v3

--- a/solution.py
+++ b/solution.py
@@ -18,10 +18,10 @@
 TAIL = (
     "S2", "D3", "S3", "X7", "E5", "P0", "P1", "E6", "S4", "R0", "P2", "D5", "S5", "R1",
     "E7", "P3", "S6", "R2", "N0", "P4", "D7", "S7", "R3", "N1", "P5", "R4", "N2", "R5",
-    "P6", "N3", "R6", "O0", "P7", "R7", "N4", "F0", "F1", "O1", "N5", "F2", "F3", "O2",
-    "N6", "F4", "Q0", "N7", "F5", "O3", "Q1", "F6", "F7", "M0", "O4", "Q2", "M1", "G0",
-    "O5", "Q3", "M2", "G1", "O6", "Q4", "M3", "G2", "O7", "Q5", "M4", "G3", "Q6", "M5",
-    "G4", "Q7", "M6", "G5", "M7", "G6", "G7",
+    "P6", "N3", "R6", "O0", "P7", "R7", "N4", "O1", "F0", "F1", "N5", "O2", "Q0", "F2",
+    "F3", "N6", "O3", "Q1", "F4", "F5", "N7", "O4", "Q2", "F6", "F7", "M0", "O5", "Q3",
+    "M1", "G0", "O6", "Q4", "M2", "G1", "O7", "Q5", "M3", "G2", "Q6", "M4", "G3", "M5",
+    "Q7", "G4", "M6", "G5", "M7", "G6", "G7",
 )
 NX = 4
 NY = 4
@@ -407,7 +407,8 @@
         elif kind in "FG":
             z_hi = zh if kind == "F" else 1 - zh
             project_far(k, z_hi)
-            sent_gather(k, z_hi)
+            if k >= 3:
+                sent_gather(k - 3, z_hi)
 
     @pl.when(s < n_sec - 1)
     def _():
@@ -424,6 +425,9 @@
         for j in range(1, slices, 2):
             detour_on(j).wait_send()
 
+    for k in range(slices - 3, slices):
+        for z_hi in (zh, 1 - zh):
+            sent_gather(k, z_hi)
     mean = jnp.sum(ssq[...], axis=1, keepdims=True) * jnp.float32(1.0 / (2 * NX * own))
     result = acc[...] * lax.rsqrt(mean + norm_eps)
     out[0, 0] = result[:, :BLOCK].astype(out.dtype)

time: 91.1 us -> 90.8 us (level)
  no operation moved by 1% of the time
where the time goes in v4:
time: 90.8 us; the launch traced here: 90.3 us
  Pallas kernels  88.8 us (98%)
  local copies, waits for them, and re-layouts  1.47 us (2%)
    pallas_call x1, Pallas kernels, on_device(): pl.pallas_call(kernel, out_shape=jax.ShapeDtypeStruct((1, 2, tok, kv_weig...  88.8 us

profile of v4, /device:TPU:34, one launch (start us, length us, event | category | flops | bytes accessed | tf_op | source)
XLA Modules:
  0.0 90.3 jit_solution(2954592651505000767)
XLA Ops:
  0.0 88.8 %relay.1 = bf16[1,2,128,128]{3,2,1,0:T(8,128)(2,1)} custom-call(bf16[1,1,128,16384]{3,2,1,0:T(8,128)(2,1)} %part.1, bf16[1,128,2048]{2,1,0:T(8,128)(2,1)} %resid.1, s32[1,16,128]{2,1,0:T(8,128)} %bitcast.5, s32[128,128]{1,0:T(8,128)} %bitcast.3, f32[128,128]{1,0:T(8,128)} %bitcast.4, bf16[1,2,16384,128]{3,2,1,0:T(8,128)(2,1)} %w_h.1), custom_call_target="tpu_custom_call" | custom-call | flops 3221225472 | bytes 14680064 | tf_op jit(solution)/shard_map/relay/pallas_call | solution.py:445
  88.8 1.5 %copy.8 = bf16[1,2,128,128]{3,2,1,0:T(8,128)(2,1)} copy(bf16[1,2,128,128]{3,2,1,0:T(8,128)(2,1)} %relay.1) | data formatting | bytes 131072

commit v5 on v4

--- a/solution.py
+++ b/solution.py
@@ -218,13 +218,16 @@
             near(j, d).wait_recv()
             comb(j, d).wait_recv()
         zs[j] = gathered_sum(j, 1 - zh).astype(jnp.bfloat16)
-        pair(j).start()
+
+        @pl.when(s < n_sec - 1)
+        def _():
+            pair(j).start()
 
     def row(ref, b):
         return ref[pl.ds(b, 1), :]
 
     def encode(j):
-        pair(j).wait_recv()
+        pl.when(s < n_sec - 1)(lambda: pair(j).wait_recv())
         summed = (
             gathered_sum(j, zh)
             + zr[j].astype(jnp.float32)
@@ -360,7 +363,7 @@
             far(k, d).wait_send()
             near(k, d).wait_send()
             comb(k, d).wait_send()
-        pair(k).wait_send()
+        pl.when(s < n_sec - 1)(lambda: pair(k).wait_send())
 
     def sent_gather(j, z_hi):
         forward(j, z_hi).wait_send()

time: 90.8 us -> 90.8 us (level)
  no operation moved by 1% of the time
where the time goes in v5:
time: 90.8 us; the launch traced here: 90.3 us
  Pallas kernels  88.8 us (98%)
  local copies, waits for them, and re-layouts  1.47 us (2%)
    pallas_call x1, Pallas kernels, on_device(): pl.pallas_call(kernel, out_shape=jax.ShapeDtypeStruct((1, 2, tok, kv_weig...  88.8 us

profile of v5, /device:TPU:34, one launch (start us, length us, event | category | flops | bytes accessed | tf_op | source)
XLA Modules:
  0.0 90.3 jit_solution(480317887913003215)
XLA Ops:
  0.0 88.8 %relay.1 = bf16[1,2,128,128]{3,2,1,0:T(8,128)(2,1)} custom-call(bf16[1,1,128,16384]{3,2,1,0:T(8,128)(2,1)} %part.1, bf16[1,128,2048]{2,1,0:T(8,128)(2,1)} %resid.1, s32[1,16,128]{2,1,0:T(8,128)} %bitcast.5, s32[128,128]{1,0:T(8,128)} %bitcast.3, f32[128,128]{1,0:T(8,128)} %bitcast.4, bf16[1,2,16384,128]{3,2,1,0:T(8,128)(2,1)} %w_h.1), custom_call_target="tpu_custom_call" | custom-call | flops 3221225472 | bytes 14680064 | tf_op jit(solution)/shard_map/relay/pallas_call | solution.py:448
  88.8 1.5 %copy.8 = bf16[1,2,128,128]{3,2,1,0:T(8,128)(2,1)} copy(bf16[1,2,128,128]{3,2,1,0:T(8,128)(2,1)} %relay.1) | data formatting | bytes 131072
